TPU v7x, 512 devices: a whole 4x4x16 slice. The times are simulated.
512 devices in a mesh: dp: 16 (over z), expert: 32 (over x, y, core).
Axes of the slice: x: 4, y: 4, z: 16, core: 2. Of those that a mesh axis runs over, the one named last changes fastest.
Arguments:
- cotangent: bfloat16 [65536, 1440], P(('dp', 'expert')), may hold values from -0.0625 to 0.0625
- gates: bfloat16 [65536, 4], P(('dp', 'expert')), may hold values from 0.049804688 to 0.59765625
- routes: int32 [65536, 4], P(('dp', 'expert')), may hold values from 0 to 31, as said below
- slots: int32 [65536, 4], P(('dp', 'expert')), may hold values from 0 to 31, as said below
- saved_hidden: bfloat16 [16, 32, 32, 32, 1440], P('dp', 'expert'), may hold values from -6 to 6
- left_wide: bfloat16 [32, 960, 960], P('expert', None, 'dp')
- left_narrow: bfloat16 [32, 480, 480], P('expert', None, 'dp')
- right_wide: bfloat16 [32, 960, 960], P('expert', None, 'dp')
- right_narrow: bfloat16 [32, 480, 480], P('expert', None, 'dp')
Outputs:
- precond_wide: float32 [32, 1440, 960], P('expert', None, 'dp')
- precond_narrow: float32 [32, 1440, 480], P('expert', None, 'dp')
Inputs may be any that keep to these rules, and one draw needn't show every extreme that they name: Each row names 4 different experts. On each device the experts fall into groups of four and a token's routes name one whole group; no expert is named more than 32 times by the tokens of one device, and one expert is named exactly 32 times by the tokens of every device. slots[t, k] is the row of route k of token t in the buffer of 32 rows that its device fills for that expert; the routes of one device to one expert have different slots.
All inputs are finite; a program needn't handle non-finite values.
Results may differ from a plain program's by a relative error of at most 0.024.
Values may be sent and summed in bfloat16 or wider, within the bound.
A program may use at most 64 MiB of HBM per device.

v0:
```python
import jax
import jax.numpy as jnp
from jax import lax
from jax.sharding import PartitionSpec as P


def matmul_half(left_side, right_side):
    return jnp.dot(left_side, right_side, preferred_element_type=jnp.float32)


def body(
    cotangent, gates, routes, slots, saved_hidden, left_wide, left_narrow, right_wide, right_narrow
):
    model_width = cotangent.shape[1]
    expert_count = lax.axis_size("expert")
    capacity = saved_hidden.shape[3]
    ff_width = saved_hidden.shape[4]
    block_size = left_wide.shape[1]
    scaled_rows = (
        gates.astype(jnp.float32)[:, :, None] * cotangent.astype(jnp.float32)[:, None, :]
    ).astype(jnp.bfloat16)
    target = (routes * capacity + slots).reshape(-1)
    outbound = (
        jnp.zeros((expert_count * capacity, model_width), jnp.bfloat16)
        .at[target]
        .set(scaled_rows.reshape(-1, model_width))
    )
    inbound = lax.all_to_all(
        outbound.reshape(expert_count, capacity, model_width),
        "expert",
        split_axis=0,
        concat_axis=0,
        tiled=True,
    )
    arrived = inbound.reshape(-1, model_width)
    activations = saved_hidden.reshape(-1, ff_width)
    contract = (((0,), (0,)), ((), ()))
    partial_value = lax.dot_general(
        activations, arrived, contract, preferred_element_type=jnp.float32
    )
    gradient = lax.psum(partial_value.astype(jnp.bfloat16), "dp")
    column_wide = matmul_half(gradient[:, :block_size], right_wide[0]).astype(jnp.bfloat16)
    column_narrow = matmul_half(gradient[:, block_size:], right_narrow[0]).astype(jnp.bfloat16)
    columns = jnp.concatenate([column_wide, column_narrow], axis=1)
    offset = jnp.int32(0)
    piece_wide = lax.all_gather(left_wide, "dp", axis=2, tiled=True)
    piece_narrow = lax.all_gather(left_narrow, "dp", axis=2, tiled=True)
    rows_upper = lax.dynamic_slice_in_dim(columns, offset, piece_wide.shape[2], 0)
    rows_lower = lax.dynamic_slice_in_dim(columns, block_size, piece_narrow.shape[2], 0)
    upper_rows = matmul_half(piece_wide[0], rows_upper)
    lower_rows = matmul_half(piece_narrow[0], rows_lower)
    upper_rows, lower_rows = (upper_rows, lower_rows)
    stacked = jnp.concatenate([upper_rows, lower_rows], axis=0)
    split_at = right_wide.shape[2]
    return (stacked[None, :, :split_at], stacked[None, :, split_at:])


def solution(mesh):
    return jax.shard_map(
        body,
        mesh=mesh,
        in_specs=(
            P(("dp", "expert"), None),
            P(("dp", "expert"), None),
            P(("dp", "expert"), None),
            P(("dp", "expert"), None),
            P("dp", "expert", None, None, None),
            P("expert", None, "dp"),
            P("expert", None, "dp"),
            P("expert", None, "dp"),
            P("expert", None, "dp"),
        ),
        out_specs=(P("expert", None, "dp"), P("expert", None, "dp")),
        check_vma=False,
    )
```

profile of v0, /device:TPU:24, one launch (start us, length us, event | category | flops | bytes accessed | tf_op | source)
XLA Modules:
  0.0 292.8 jit_solution(5271035906188533037)
XLA Ops:
  7.2 2.2 copy.28
  9.4 3.3 %mul.31 = f32[128,4,1440]{2,1,0:T(4,128)} broadcast(f32[128,1440]{1,0:T(8,128)} %copy.28), dimensions={0,2} | broadcast | bytes 3686400 | tf_op jit(solution)/shard_map/mul | solution.py:20
  12.7 4.9 %mul.32 = f32[512,1440]{1,0:T(8,128)} reshape(f32[128,4,1440]{2,1,0:T(4,128)} %mul.31) | data formatting | bytes 5898240 | tf_op jit(solution)/shard_map/mul | solution.py:20
  17.7 0.1 copy.26
  17.8 0.1 reshape.51
  17.9 0.1 copy.27
  18.0 0.1 reshape.55
  18.1 6.5 %scatter_custom_fusion = bf16[1024,1440]{1,0:T(8,128)(2,1)} fusion(s32[512]{0:T(512)S(1)} %bitcast.32, f32[512,1440]{1,0:T(8,128)} %mul.32, f32[512]{0:T(512)S(1)} %reshape.55, bf16[]{:T(256)} %constant.0.clone.1), kind=kCustom, calls=%fused_computation.10 | custom fusion | flops 1474560 | bytes 5900290 | tf_op jit(solution)/shard_map/scatter | solution.py:26
  24.6 10.2 %all-to-all-start = ((bf16[32,32,1440]{2,1,0:T(8,128)(2,1)}), bf16[32,32,1440]{2,1,0:T(8,128)(2,1)}, u32[]{:S(2)}, u32[]{:S(2)}) async-start(bf16[32,32,1440]{2,1,0:T(8,128)(2,1)} %bitcast.31), calls=%async_computation | async-start | bytes 6291456 | tf_op jit(solution)/shard_map/all_to_all | solution.py:28
  34.8 0.9 copy.29
  35.8 37.3 %all-to-all-done = bf16[32,32,1440]{2,1,0:T(8,128)(2,1)} async-done(((bf16[32,32,1440]{2,1,0:T(8,128)(2,1)}), bf16[32,32,1440]{2,1,0:T(8,128)(2,1)}, u32[]{:S(2)}, u32[]{:S(2)}) %all-to-all-start) | async-done | bytes 2949152 | tf_op jit(solution)/shard_map/all_to_all | solution.py:28
  73.1 8.5 %fusion = bf16[1440,1440]{0,1:T(8,128)(2,1)} fusion(bf16[1024,1440]{1,0:T(8,128)(2,1)} %bitcast.2, bf16[1024,1440]{1,0:T(8,128)(2,1)S(1)} %bitcast.30), kind=kOutput, calls=%fused_computation.2 | convolution fusion | flops 4248806400 | bytes 10045440 | tf_op jit(solution)/shard_map/dot_general | solution.py:38
  81.6 0.7 copy-done.4
  82.3 45.9 %all_gather.7 = bf16[1,480,480]{1,0,2:T(2,128)(2,1)} all-gather(bf16[1,480,30]{1,0,2:T(2,128)(2,1)S(1)} %copy.31), channel_id=1, replica_groups=mesh['dp'=16,'expert'=32] {'dp'}, dimensions={2}, use_global_device_ids=true | all-gather | bytes 489600 | tf_op jit(solution)/shard_map/all_gather | solution.py:47
  128.2 3.5 %copy.32 = bf16[1,480,480]{2,1,0:T(8,128)(2,1)} copy(bf16[1,480,480]{1,0,2:T(2,128)(2,1)} %all_gather.7) | data formatting | bytes 921600 | tf_op jit(solution)/shard_map/all_gather | solution.py:47
  131.7 10.6 %copy.30 = bf16[1,960,960]{2,1,0:T(8,128)(2,1)} copy(bf16[1,960,960]{1,0,2:T(2,128)(2,1)} %all-gather.2.cloned.1.call-done) | data formatting | bytes 3686400 | tf_op jit(solution)/shard_map/all_gather | solution.py:46
  142.3 136.0 %all-reduce.2.cloned.1.call-done = bf16[1440,1440]{0,1:T(8,128)(2,1)} async-done(((bf16[1440,1440]{0,1:T(8,128)(2,1)}), bf16[1440,1440]{0,1:T(8,128)(2,1)}) %all-reduce.2.cloned.1.call-update) | async-done | bytes 4147216 | tf_op jit(solution)/shard_map/psum | solution.py:41
  278.3 2.5 fusion.3
  280.8 1.9 convolution_convert_fusion.1
  282.7 0.3 convolution_bitcast_fusion
  283.0 0.7 fusion.12
  283.9 0.1 fusion.17
  284.0 0.9 copy.34
  284.8 1.1 copy.33
  (28 shorter events, 0.3 us)
Async XLA Ops:
  7.2 65.9 %copy-start = (bf16[1,1,32,32,1440]{4,3,2,1,0:T(8,128)(2,1)S(1)}, bf16[1,1,32,32,1440]{4,3,2,1,0:T(8,128)(2,1)}, u32[]{:S(2)}) copy-start(bf16[1,1,32,32,1440]{4,3,2,1,0:T(8,128)(2,1)} %param.13) | copy-start | bytes 8847364
  12.7 4.9 %copy-start.5 = (s32[128,4]{0,1:T(4,128)S(1)}, s32[128,4]{0,1:T(4,128)}, u32[]{:S(2)}) copy-start(s32[128,4]{0,1:T(4,128)} %param.12) | copy-start | bytes 6148
  12.7 4.9 %copy-start.6 = (s32[128,4]{0,1:T(4,128)S(1)}, s32[128,4]{0,1:T(4,128)}, u32[]{:S(2)}) copy-start(s32[128,4]{0,1:T(4,128)} %param.11) | copy-start | bytes 6148
  12.7 5.2 %copy-start.7 = (bf16[128,4]{0,1:T(4,128)(2,1)S(1)}, bf16[128,4]{0,1:T(4,128)(2,1)}, u32[]{:S(2)}) copy-start(bf16[128,4]{0,1:T(4,128)(2,1)} %param.10) | copy-start | bytes 3076
  24.6 10.2 %copy-start.3 = (bf16[1,960,60]{1,2,0:T(8,128)(2,1)S(1)}, bf16[1,960,60]{1,2,0:T(8,128)(2,1)}, u32[]{:S(2)}) copy-start(bf16[1,960,60]{1,2,0:T(8,128)(2,1)} %param.14) | copy-start | bytes 345604
  24.6 48.5 %all-to-all-start = ((bf16[32,32,1440]{2,1,0:T(8,128)(2,1)}), bf16[32,32,1440]{2,1,0:T(8,128)(2,1)}, u32[]{:S(2)}, u32[]{:S(2)}) async-start(bf16[32,32,1440]{2,1,0:T(8,128)(2,1)} %bitcast.31), calls=%async_computation | async-start | bytes 6291456 | tf_op jit(solution)/shard_map/all_to_all | solution.py:28
  34.8 96.9 %all-gather.2.cloned.1.call-start = ((), (), s32[]{:S(2)}) async-start(), calls=%async_computation.2 | async-start | bytes 4177920 | tf_op jit(solution)/shard_map/all_gather | solution.py:46
  35.7 242.5 %all-reduce.2.cloned.1.call-start = ((), (), s32[]{:S(2)}) async-start(), calls=%async_computation.1 | async-start | bytes 8847360 | tf_op jit(solution)/shard_map/psum | solution.py:41
  81.5 0.8 copy-start.4
  131.7 146.6 %copy-start.8 = (bf16[1,960,60]{1,2,0:T(8,128)(2,1)S(1)}, bf16[1,960,60]{1,2,0:T(8,128)(2,1)}, u32[]{:S(2)}) copy-start(bf16[1,960,60]{1,2,0:T(8,128)(2,1)} %param.16) | copy-start | bytes 345604
  142.3 138.5 %copy-start.9 = (bf16[1,480,30]{1,2,0:T(8,128)(2,1)S(1)}, bf16[1,480,30]{1,2,0:T(8,128)(2,1)}, u32[]{:S(2)}) copy-start(bf16[1,480,30]{1,2,0:T(8,128)(2,1)} %param.17) | copy-start | bytes 86404
  278.3 4.4 %copy-start.2 = (bf16[1,480,480]{2,1,0:T(8,128)(2,1)S(1)}, bf16[1,480,480]{2,1,0:T(8,128)(2,1)}, u32[]{:S(2)}) copy-start(bf16[1,480,480]{2,1,0:T(8,128)(2,1)} %copy.32) | copy-start | bytes 1382404
  280.8 2.2 copy-start.1
Sparse Core Ops, SparseCore 0:
  38.3 83.2 all-gather.1
  123.9 154.3 all-reduce.1
where the time goes:
time: 294 us; the launch traced here: 293 us
  waiting for transfers between devices  173 us (59%)
  blocking collectives  45.9 us (16%)
  local copies, waits for them, and re-layouts  28.6 us (10%)
  between operations  14.2 us (5%)
  matrix products  13.9 us (5%)
  starting transfers between devices  10.2 us (3%)
  other arithmetic  6.69 us (2%)
    psum x1, waiting for transfers between devices, body(): gradient = lax.psum(partial_value.astype(jnp.bfloat16), 'dp')  136 us
    all_gather x1, blocking collectives, body(): piece_narrow = lax.all_gather(left_narrow, 'dp', axis=2, tiled=True)  45.9 us
    all_to_all x1, waiting for transfers between devices, body(): lax.all_to_all(outbound.reshape(expert_count, capacity, model_width), 'ex...  37.3 us
    all_gather x1, local copies, waits for them, and re-layouts, body(): piece_wide = lax.all_gather(left_wide, 'dp', axis=2, tiled=True)  10.6 us
    all_to_all x1, starting transfers between devices, body(): lax.all_to_all(outbound.reshape(expert_count, capacity, model_width), 'ex...  10.2 us
    dot_general x1, matrix products, body(): lax.dot_general(activations, arrived, contract, preferred_element_type=jn...  8.48 us
    mul x4, local copies, waits for them, and re-layouts, body(): gates.astype(jnp.float32)[:, :, None]  8.46 us
    scatter x1, other arithmetic, body(): outbound = jnp.zeros((expert_count * capacity, model_width), jnp.bfloat16...  6.48 us
  transfers between devices with their start and end apart: 3, of which 2 were waited for; matrix products, arithmetic and copies ran while one was open for 8% of the time, Pallas kernels for 0%

commit v1 on v0

v1 whole, which is shorter than its diff:
```python
import functools

import jax
import jax.numpy as jnp
from jax import lax
from jax.experimental import pallas as pl
from jax.experimental.pallas import tpu as pltpu
from jax.sharding import PartitionSpec as P

MESH = pl.DeviceIdType.MESH
BF = jnp.bfloat16
F32 = jnp.float32
LANE = 128


def up(value, unit):
    return -(-value // unit) * unit


def nn(left, right):
    return lax.dot_general(left, right, (((1,), (0,)), ((), ())), preferred_element_type=F32)


def nt(left, right):
    return lax.dot_general(left, right, (((1,), (1,)), ((), ())), preferred_element_type=F32)


class Sizes:
    def __init__(self, ring, experts, capacity, width, wide, narrow, tokens, routes):
        self.ring, self.experts, self.capacity = ring, experts, capacity
        self.width, self.wide, self.narrow = width, wide, narrow
        self.tokens, self.routes = tokens, routes
        self.wp, self.np = up(wide, LANE), up(narrow, LANE)
        self.full = self.wp + self.np
        self.cw, self.cn = wide // ring, narrow // ring
        self.cwp, self.cnp = up(self.cw, 32), up(self.cn, 32)
        self.seg = self.cwp + self.cnp
        self.half = ring // 2
        self.rows = experts * capacity
        self.kchunks = min(4, experts)
        self.kblocks = experts // self.kchunks
        self.krows = self.kblocks * capacity
        self.tile = min(256, self.np)


def kernel(
    z, cot_ref, gates_ref, routes_ref, slots_ref, hid_hbm, lw_ref, ln_ref, rw_ref, rn_ref,
    ow_ref, on_ref,
    hid_v, at, cotp, outb, inb, acc, part, rtw, rtn, ltw, ltn, ht, land, lwc, lnc,
    hid_sem, a2a_send, a2a_recv, ag_send, ag_recv, rs_send, rs_recv,
):
    n, half, experts = z.ring, z.half, z.experts
    zi = lax.axis_index("dp")
    ei = lax.axis_index("expert")
    plus = (lax.rem(zi + 1, n), ei)
    minus = (lax.rem(zi + n - 1, n), ei)
    neighbour = (plus, minus)

    barrier = pltpu.get_barrier_semaphore()
    for target in neighbour:
        pl.semaphore_signal(barrier, inc=1, device_id=target, device_id_type=MESH)

    def greet(k, carry):
        pl.semaphore_signal(
            barrier, inc=1, device_id=(zi, lax.rem(ei + k, experts)), device_id_type=MESH
        )
        return carry

    lax.fori_loop(1, experts, greet, 0)

    def hidden_copy(k):
        return pltpu.make_async_copy(
            hid_hbm.at[lax.rem(ei + k, experts)], hid_v.at[k], hid_sem.at[k]
        )

    def hidden_start(k, carry):
        hidden_copy(k).start()
        return carry

    lax.fori_loop(0, experts, hidden_start, 0)

    for dst, src, rows, cols in (
        (rtw, rw_ref, z.cw, z.wide), (rtn, rn_ref, z.cn, z.narrow),
        (ltw, lw_ref, z.cw, z.wide), (ltn, ln_ref, z.cn, z.narrow),
    ):
        dst[0] = jnp.zeros(dst.shape[1:], BF)
        dst[0, :rows, :cols] = src[...]

    cotp[...] = jnp.zeros_like(cotp)
    cotp[: z.wide, :] = cot_ref[: z.wide, :]
    cotp[z.wp : z.wp + z.narrow, :] = cot_ref[z.wide :, :]
    place = routes_ref[...] * z.capacity + slots_ref[...]
    gate = gates_ref[...].astype(F32)

    def build(block, carry):
        row = lax.broadcasted_iota(jnp.int32, (z.krows, z.tokens), 0) + block * z.krows
        weight = jnp.zeros((z.krows, z.tokens), F32)
        for k in range(z.routes):
            weight = weight + jnp.where(row == place[k : k + 1, :], gate[k : k + 1, :], 0.0)
        rows = nt(weight.astype(BF), cotp[...]).astype(BF)
        outb[pl.ds(block * z.kblocks, z.kblocks)] = rows.reshape(z.kblocks, z.capacity, z.full)
        return carry

    lax.fori_loop(0, z.kchunks, build, 0)

    pl.semaphore_wait(barrier, experts + 1)

    def gather_copies(kind, direction, step):
        copies = []
        for piece, buf in enumerate(((rtw, rtn), (ltw, ltn))[kind]):
            if direction == 0:
                src, dst = (n - step + 1) % n, n - step
            else:
                src, dst = step - 1, step
            src_ref, dst_ref = buf.at[src], buf.at[dst]
            if step == half:
                middle = buf.shape[1] // 2
                rows = pl.ds(direction * middle, middle)
                src_ref, dst_ref = buf.at[src, rows], buf.at[dst, rows]
            copies.append(pltpu.make_async_remote_copy(
                src_ref=src_ref, dst_ref=dst_ref,
                send_sem=ag_send.at[kind, direction, step - 1, piece],
                recv_sem=ag_recv.at[kind, direction, step - 1, piece],
                device_id=neighbour[direction], device_id_type=MESH,
            ))
        return copies

    def gather_start(kind, step):
        for direction in range(2):
            for copy in gather_copies(kind, direction, step):
                copy.start()

    def gather_step(kind, step):
        for direction in range(2):
            for copy in gather_copies(kind, direction, step):
                copy.wait_recv()
            if step < half:
                for copy in gather_copies(kind, direction, step + 1):
                    copy.start()

    gather_start(0, 1)

    def routed_copy(k):
        partner = lax.rem(ei + experts - k, experts)
        return pltpu.make_async_remote_copy(
            src_ref=outb.at[partner], dst_ref=inb.at[k],
            send_sem=a2a_send.at[k], recv_sem=a2a_recv.at[k],
            device_id=(zi, partner), device_id_type=MESH,
        )

    def routed_start(k, carry):
        routed_copy(k).start()
        return carry

    lax.fori_loop(1, experts, routed_start, 0)
    gather_start(1, 1)
    inb[0] = outb[ei]

    def hidden_wait(k, carry):
        hidden_copy(k).wait()
        return carry

    lax.fori_loop(0, experts, hidden_wait, 0)

    at[z.wide : z.wp, :] = jnp.zeros((z.wp - z.wide, z.rows), BF)
    at[z.wp + z.narrow :, :] = jnp.zeros((z.np - z.narrow, z.rows), BF)
    for first in range(0, z.width, LANE):
        size = min(LANE, z.width - first)
        turned = hid_v[:, :, first : first + size].reshape(z.rows, size).T
        cut = min(max(z.wide - first, 0), size)
        if cut > 0:
            at[first : first + cut, :] = turned[:cut]
        if cut < size:
            base = first + cut - z.wide + z.wp
            at[base : base + size - cut, :] = turned[cut:]

    def accumulate(chunk):
        def arrived(k, carry):
            routed_copy(k).wait_recv()
            return carry

        lax.fori_loop(max(chunk * z.kblocks, 1), (chunk + 1) * z.kblocks, arrived, 0)

        def tile(m, carry):
            rows = pl.ds(pl.multiple_of(m * z.tile, z.tile), z.tile)
            piece = inb[chunk * z.kblocks : (chunk + 1) * z.kblocks].reshape(z.krows, z.full)
            value = nn(at[rows, chunk * z.krows : (chunk + 1) * z.krows], piece)
            if chunk > 0:
                value = value + acc[rows, :]
            if chunk < z.kchunks - 1:
                acc[rows, :] = value
            else:
                part[rows, :] = value.astype(BF)
            return carry

        lax.fori_loop(0, z.full // z.tile, tile, 0)

    def right(first, count):
        def tile(m, carry):
            cols = pl.ds(pl.multiple_of(m * z.tile, z.tile), z.tile)
            wide = nt(rtw[first : first + count].reshape(count * z.cwp, z.wp), part[cols, : z.wp])
            narrow = nt(rtn[first : first + count].reshape(count * z.cnp, z.np), part[cols, z.wp :])
            ht[first : first + count, : z.cwp, cols] = wide.astype(BF).reshape(count, z.cwp, z.tile)
            ht[first : first + count, z.cwp :, cols] = narrow.astype(BF).reshape(count, z.cnp, z.tile)
            return carry

        lax.fori_loop(0, z.full // z.tile, tile, 0)

    late = {half - 3 + c: c for c in range(z.kchunks)} if half >= 8 else {}
    for step in range(1, half + 1):
        gather_step(0, step)
        gather_step(1, step)
        if step in late:
            accumulate(late[step])
    for chunk in range(z.kchunks):
        if chunk not in late.values():
            accumulate(chunk)

    middle = z.seg // 2

    def hops(direction, piece):
        return half if direction == piece else half - 1

    def own_slot(direction, distance):
        return distance if direction == 0 else (n - distance) % n

    def reduce_copy(direction, piece, hop):
        rows = pl.ds(piece * middle, middle)
        if hop == 1:
            src = ht.at[own_slot(direction, hops(direction, piece)), rows]
        else:
            src = land.at[direction, hop - 2, rows]
        return pltpu.make_async_remote_copy(
            src_ref=src, dst_ref=land.at[direction, hop - 1, rows],
            send_sem=rs_send.at[direction, piece, hop - 1],
            recv_sem=rs_recv.at[direction, piece, hop - 1],
            device_id=neighbour[direction], device_id_type=MESH,
        )

    group = max(1, n // 4)
    start = half - group // 2
    right(start, group)
    lanes = ((0, 0), (1, 1), (0, 1), (1, 0))
    for direction, piece in lanes:
        reduce_copy(direction, piece, 1).start()
    right(start + group, group)
    right(start - group, group)

    def reduce_step(hop):
        for direction, piece in lanes:
            if hop >= hops(direction, piece):
                continue
            reduce_copy(direction, piece, hop).wait_recv()
            rows = slice(piece * middle, (piece + 1) * middle)
            slot = own_slot(direction, hops(direction, piece) - hop)
            total = land[direction, hop - 1, rows].astype(F32) + ht[slot, rows].astype(F32)
            land[direction, hop - 1, rows] = total.astype(BF)
            reduce_copy(direction, piece, hop + 1).start()

    def compact(dst, src, count, unit, valid):
        shift = unit.bit_length() - 1
        depth = n * unit

        def tile(m, carry):
            rows = pl.ds(pl.multiple_of(m * z.tile, z.tile), z.tile)
            feature = lax.broadcasted_iota(jnp.int32, (z.tile, depth), 0) + m * z.tile
            place = lax.broadcasted_iota(jnp.int32, (z.tile, depth), 1)
            owner = (zi + lax.shift_right_logical(place, shift)) & (n - 1)
            inner = place & (unit - 1)
            pick = jnp.where((feature == owner * valid + inner) & (inner < valid), 1.0, 0.0)
            dst[rows, :] = nn(pick.astype(BF), src[...].reshape(depth, src.shape[2])).astype(BF)
            return carry

        lax.fori_loop(0, count // z.tile, tile, 0)

    for hop in range(1, half):
        reduce_step(hop)
        if hop == 1:
            if start + 2 * group < n:
                right(start + 2 * group, n - start - 2 * group)
            if start - group > 0:
                right(0, start - group)
            compact(lwc, ltw, z.wp, z.cwp, z.cw)
            compact(lnc, ltn, z.np, z.cnp, z.cn)

    sums = []
    for piece in range(2):
        rows = slice(piece * middle, (piece + 1) * middle)
        total = ht[0, rows].astype(F32)
        for direction in range(2):
            hop = hops(direction, piece)
            reduce_copy(direction, piece, hop).wait_recv()
            total = total + land[direction, hop - 1, rows].astype(F32)
        sums.append(total.astype(BF))
    final = jnp.concatenate(sums, axis=0)
    upper = nn(final[:, : z.wp], lwc[...])
    lower = nn(final[:, z.wp :], lnc[...])
    ow_ref[:, : z.wide] = upper[: z.cw, : z.wide]
    ow_ref[:, z.wide :] = lower[: z.cw, : z.narrow]
    on_ref[:, : z.wide] = upper[z.cwp : z.cwp + z.cn, : z.wide]
    on_ref[:, z.wide :] = lower[z.cwp : z.cwp + z.cn, : z.narrow]

    def routed_sent(k, carry):
        routed_copy(k).wait_send()
        return carry

    lax.fori_loop(1, experts, routed_sent, 0)
    for kind in range(2):
        for step in range(1, half + 1):
            for direction in range(2):
                for copy in gather_copies(kind, direction, step):
                    copy.wait_send()
    for direction, piece in lanes:
        for hop in range(1, hops(direction, piece) + 1):
            reduce_copy(direction, piece, hop).wait_send()


def body(
    cotangent, gates, routes, slots, saved_hidden, left_wide, left_narrow, right_wide, right_narrow
):
    ring, experts = lax.axis_size("dp"), lax.axis_size("expert")
    capacity, width = saved_hidden.shape[3:]
    z = Sizes(
        ring, experts, capacity, width, left_wide.shape[1], left_narrow.shape[1],
        cotangent.shape[0], gates.shape[1],
    )
    vmem = pl.BlockSpec(memory_space=pltpu.VMEM)
    ow, on = pl.pallas_call(
        functools.partial(kernel, z),
        out_shape=(
            jax.ShapeDtypeStruct((z.cw, z.width), F32),
            jax.ShapeDtypeStruct((z.cn, z.width), F32),
        ),
        in_specs=[vmem] * 4 + [pl.BlockSpec(memory_space=pl.ANY)] + [vmem] * 4,
        out_specs=(vmem, vmem),
        scratch_shapes=[
            pltpu.VMEM((experts, capacity, width), BF),
            pltpu.VMEM((z.full, z.rows), BF),
            pltpu.VMEM((z.full, z.tokens), BF),
            pltpu.VMEM((experts, capacity, z.full), BF),
            pltpu.VMEM((experts, capacity, z.full), BF),
            pltpu.VMEM((z.full, z.full), F32),
            pltpu.VMEM((z.full, z.full), BF),
            pltpu.VMEM((ring, z.cwp, z.wp), BF),
            pltpu.VMEM((ring, z.cnp, z.np), BF),
            pltpu.VMEM((ring, z.cwp, z.wp), BF),
            pltpu.VMEM((ring, z.cnp, z.np), BF),
            pltpu.VMEM((ring, z.seg, z.full), BF),
            pltpu.VMEM((2, z.half, z.seg, z.full), BF),
            pltpu.VMEM((z.wp, z.wp), BF),
            pltpu.VMEM((z.np, z.np), BF),
            pltpu.SemaphoreType.DMA((experts,)),
            pltpu.SemaphoreType.DMA((experts,)),
            pltpu.SemaphoreType.DMA((experts,)),
            pltpu.SemaphoreType.DMA((2, 2, z.half, 2)),
            pltpu.SemaphoreType.DMA((2, 2, z.half, 2)),
            pltpu.SemaphoreType.DMA((2, 2, z.half)),
            pltpu.SemaphoreType.DMA((2, 2, z.half)),
        ],
        compiler_params=pltpu.CompilerParams(
            collective_id=0, has_side_effects=True, vmem_limit_bytes=60 * 1024 * 1024
        ),
        cost_estimate=pl.CostEstimate(flops=10_000_000_000, bytes_accessed=8_000_000, transcendentals=0),
    )(
        cotangent.T, gates.T, routes.T, slots.T,
        saved_hidden.reshape(experts, capacity, width),
        left_wide[0].T, left_narrow[0].T, right_wide[0].T, right_narrow[0].T,
    )
    return ow.T[None], on.T[None]


def solution(mesh):
    return jax.shard_map(
        body,
        mesh=mesh,
        in_specs=(
            P(("dp", "expert"), None),
            P(("dp", "expert"), None),
            P(("dp", "expert"), None),
            P(("dp", "expert"), None),
            P("dp", "expert", None, None, None),
            P("expert", None, "dp"),
            P("expert", None, "dp"),
            P("expert", None, "dp"),
            P("expert", None, "dp"),
        ),
        out_specs=(P("expert", None, "dp"), P("expert", None, "dp")),
        check_vma=False,
    )
```

time: 294 us -> 159 us (0.54)
  the two profiles are of different devices: /device:TPU:24 before, /device:TPU:3 now
where the time goes in v1:
time: 159 us; the launch traced here: 158 us
  Pallas kernels  154 us (97%)
  local copies, waits for them, and re-layouts  3.9 us (2%)
    pallas_call x1, Pallas kernels, body(): pl.pallas_call(functools.partial(kernel, z), out_shape=(jax.ShapeDtypeStr...  154 us
    unnamed x2, local copies, waits for them, and re-layouts  3.9 us

profile of v1, /device:TPU:3, one launch (start us, length us, event | category | flops | bytes accessed | tf_op | source)
XLA Modules:
  0.0 158.5 jit_solution(18130583351197125705)
XLA Ops:
  0.6 153.9 %shard_map.104 = (f32[60,1440]{1,0:T(8,128)}, f32[30,1440]{1,0:T(8,128)}) custom-call(bf16[1440,128]{1,0:T(8,128)(2,1)} %bitcast.26, bf16[4,128]{1,0:T(4,128)(2,1)} %bitcast.33, s32[4,128]{1,0:T(4,128)} %bitcast.31, s32[4,128]{1,0:T(4,128)} %bitcast.32, bf16[32,32,1440]{2,1,0:T(8,128)(2,1)} %bitcast.25, bf16[60,960]{1,0:T(8,128)(2,1)} %bitcast.27, ...), custom_call_target="tpu_custom_call" | custom-call | flops 10000000000 | bytes 8000000 | tf_op jit(solution)/shard_map/pallas_call | solution.py:328
  154.6 2.1 %copy.11 = f32[1,1440,60]{1,0,2:T(1,128)} copy(f32[1,1440,60]{1,2,0:T(8,128)} %bitcast.23) | data formatting | bytes 691200
  156.7 1.8 %copy.12 = f32[1,1440,30]{1,0,2:T(1,128)} copy(f32[1,1440,30]{1,2,0:T(8,128)} %bitcast.24) | data formatting | bytes 345600

commit v2 on v1

v2 whole, which is shorter than its diff:
```python
import functools
import math

import jax
import jax.numpy as jnp
from jax import lax
from jax.experimental import pallas as pl
from jax.experimental.pallas import tpu as pltpu
from jax.sharding import PartitionSpec as P

MESH = pl.DeviceIdType.MESH
BF = jnp.bfloat16
F32 = jnp.float32
LANE = 128


def up(value, unit):
    return -(-value // unit) * unit


def nn(left, right):
    return lax.dot_general(left, right, (((1,), (0,)), ((), ())), preferred_element_type=F32)


def nt(left, right):
    return lax.dot_general(left, right, (((1,), (1,)), ((), ())), preferred_element_type=F32)


class Sizes:
    def __init__(self, ring, experts, capacity, width, wide, narrow, tokens, routes):
        self.ring, self.experts, self.capacity = ring, experts, capacity
        self.width, self.wide, self.narrow = width, wide, narrow
        self.tokens, self.routes = tokens, routes
        self.cw, self.cn = wide // ring, narrow // ring
        self.cwp, self.cnp = up(self.cw, 32), up(self.cn, 32)
        self.seg = self.cwp + self.cnp
        self.half = ring // 2
        self.side = math.isqrt(experts // 2)
        self.part = width // 2
        self.meta = up(3 * routes, 16)
        self.rows = self.meta + self.part
        self.sources = 2 * self.side
        self.depth = self.sources * capacity
        self.mtile = self.part // 3
        self.pick = narrow // 2


def kernel(
    z, cot_ref, gates_ref, routes_ref, slots_ref, hid_hbm, lw_ref, ln_ref, rw_ref, rn_ref,
    ow_ref, on_ref,
    hid_v, cg, wt, acc, part, rtw, rtn, ltw, ltn, ht, land, lwc, lnc,
    hid_sem, p_send, p_recv, q_send, q_recv, s_send, s_recv, ag_send, ag_recv, rs_send, rs_recv,
):
    n, half, side = z.ring, z.half, z.side
    zi = lax.axis_index("dp")
    ei = lax.axis_index("expert")
    core = lax.rem(ei, 2)
    yi = lax.rem(ei // 2, side)
    xi = ei // (2 * side)

    def expert_at(x, y, c):
        return (x * side + y) * 2 + c

    def step_to(index, direction):
        return lax.rem(index + (1 if direction == 0 else side - 1), side)

    ring_to = ((lax.rem(zi + 1, n), ei), (lax.rem(zi + n - 1, n), ei))
    x_to = tuple((zi, expert_at(step_to(xi, d), yi, core)) for d in range(2))
    y_to = tuple((zi, expert_at(xi, step_to(yi, d), core)) for d in range(2))
    sibling = (zi, expert_at(xi, yi, 1 - core))
    axis_to = (x_to, y_to)

    barrier = pltpu.get_barrier_semaphore()
    for target in (*ring_to, *x_to, *y_to, sibling):
        pl.semaphore_signal(barrier, inc=1, device_id=target, device_id_type=MESH)

    def hidden_copy(k):
        dx, dy, dc = k // (2 * side), lax.rem(k // 2, side), lax.rem(k, 2)
        source = expert_at(
            lax.rem(xi + dx, side), lax.rem(yi + dy, side), lax.rem(core + dc, 2)
        )
        return pltpu.make_async_copy(hid_hbm.at[source], hid_v.at[dx, dy, dc], hid_sem.at[k])

    def hidden_start(k, carry):
        hidden_copy(k).start()
        return carry

    lax.fori_loop(0, z.experts, hidden_start, 0)

    for dst, src, rows in (
        (rtw, rw_ref, z.cw), (rtn, rn_ref, z.cn), (ltw, lw_ref, z.cw), (ltn, ln_ref, z.cn)
    ):
        dst[0] = jnp.zeros(dst.shape[1:], BF)
        dst[0, :rows] = src[...]
    spare = jnp.zeros((z.meta - 3 * z.routes, z.tokens), F32)
    meta = jnp.concatenate(
        [gates_ref[...].astype(F32), routes_ref[...].astype(F32), slots_ref[...].astype(F32), spare],
        axis=0,
    ).astype(BF)
    for h in range(2):
        cg[h, 0, 0, 0, : z.meta] = meta
        cg[h, 0, 0, 0, z.meta :] = cot_ref[h * z.part : (h + 1) * z.part]
    wt[...] = jnp.zeros_like(wt)

    pl.semaphore_wait(barrier, 7)

    def gather_copies(kind, direction, step):
        copies = []
        for piece, buf in enumerate(((rtw, rtn), (ltw, ltn))[kind]):
            if direction == 0:
                src, dst = (n - step + 1) % n, n - step
            else:
                src, dst = step - 1, step
            src_ref, dst_ref = buf.at[src], buf.at[dst]
            if step == half:
                middle = buf.shape[1] // 2
                rows = pl.ds(direction * middle, middle)
                src_ref, dst_ref = buf.at[src, rows], buf.at[dst, rows]
            copies.append(pltpu.make_async_remote_copy(
                src_ref=src_ref, dst_ref=dst_ref,
                send_sem=ag_send.at[kind, direction, step - 1, piece],
                recv_sem=ag_recv.at[kind, direction, step - 1, piece],
                device_id=ring_to[direction], device_id_type=MESH,
            ))
        return copies

    def gather_start(kind, step):
        for direction in range(2):
            for copy in gather_copies(kind, direction, step):
                copy.start()

    def gather_step(kind, step):
        for direction in range(2):
            for copy in gather_copies(kind, direction, step):
                copy.wait_recv()
            if step < half:
                for copy in gather_copies(kind, direction, step + 1):
                    copy.start()

    def came_from(direction):
        return side - 1 if direction == 0 else 1

    def share(direction):
        return pl.ds(direction * (z.rows // 2), z.rows // 2)

    def first_copy(h, stage, direction):
        if stage == 0:
            src, dst = cg.at[h, 0, 0, 0], cg.at[h, came_from(direction), 0, 0]
        else:
            src = cg.at[h, came_from(direction), 0, 0, share(direction)]
            dst = cg.at[h, 2, 0, 0, share(direction)]
        return pltpu.make_async_remote_copy(
            src_ref=src, dst_ref=dst,
            send_sem=p_send.at[h, stage, direction], recv_sem=p_recv.at[h, stage, direction],
            device_id=axis_to[h][direction], device_id_type=MESH,
        )

    def second_copy(h, stage, i, direction):
        if stage == 0:
            src, dst = cg.at[h, i, 0, 0], cg.at[h, i, came_from(direction), 0]
        else:
            src = cg.at[h, i, came_from(direction), 0, share(direction)]
            dst = cg.at[h, i, 2, 0, share(direction)]
        return pltpu.make_async_remote_copy(
            src_ref=src, dst_ref=dst,
            send_sem=q_send.at[h, stage, i, direction], recv_sem=q_recv.at[h, stage, i, direction],
            device_id=axis_to[1 - h][direction], device_id_type=MESH,
        )

    def sibling_copy(h, i, j):
        return pltpu.make_async_remote_copy(
            src_ref=cg.at[h, i, j, 0], dst_ref=cg.at[h, i, j, 1],
            send_sem=s_send.at[h, i, j], recv_sem=s_recv.at[h, i, j],
            device_id=sibling, device_id_type=MESH,
        )

    both = tuple((h, d) for d in range(2) for h in range(2))

    def first_arrived():
        for h, d in both:
            first_copy(h, 0, d).wait_recv()
            first_copy(h, 1, d).start()
            i = came_from(d)
            for e in range(2):
                second_copy(h, 0, i, e).start()
            sibling_copy(h, i, 0).start()

    def first_far_arrived():
        for h in range(2):
            for d in range(2):
                first_copy(h, 1, d).wait_recv()
            for e in range(2):
                second_copy(h, 0, 2, e).start()
            sibling_copy(h, 2, 0).start()

    def second_arrived(i):
        for h, d in both:
            second_copy(h, 0, i, d).wait_recv()
            second_copy(h, 1, i, d).start()
            sibling_copy(h, i, came_from(d)).start()

    def second_far_arrived(i):
        for h in range(2):
            for d in range(2):
                second_copy(h, 1, i, d).wait_recv()
            sibling_copy(h, i, 2).start()

    gather_start(0, 1)
    for h, d in both:
        first_copy(h, 0, d).start()
    for h, d in both:
        second_copy(h, 0, 0, d).start()
    gather_start(1, 1)
    for h in range(2):
        sibling_copy(h, 0, 0).start()

    def hidden_wait(k, carry):
        hidden_copy(k).wait()
        return carry

    lax.fori_loop(0, z.experts, hidden_wait, 0)

    def accumulate(h, j, is_first, is_last):
        for i in range(side):
            sibling_copy(h, i, j).wait_recv()
        place = lax.broadcasted_iota(jnp.int32, (z.capacity, z.tokens), 0).astype(F32)
        mine = ei.astype(F32)
        for s in range(z.sources):
            info = cg[h, s // 2, j, s % 2, : z.meta].astype(F32)
            weight = jnp.zeros((z.capacity, z.tokens), F32)
            for k in range(z.routes):
                gate = info[k : k + 1]
                route = info[z.routes + k : z.routes + k + 1]
                slot = info[2 * z.routes + k : 2 * z.routes + k + 1]
                weight = weight + jnp.where((route == mine) & (slot == place), gate, 0.0)
            wt[
                s * z.capacity : (s + 1) * z.capacity, s * z.tokens : (s + 1) * z.tokens
            ] = weight.astype(BF)

        def tile(m, carry):
            inner = pl.ds(pl.multiple_of(z.meta + m * z.mtile, 16), z.mtile)
            rows = pl.ds(pl.multiple_of(h * z.part + m * z.mtile, 16), z.mtile)
            left = jnp.concatenate(
                [cg[h, s // 2, j, s % 2, inner, :] for s in range(z.sources)], axis=1
            )
            routed = nt(left, wt[...]).astype(BF)
            hidden = hid_v[:, j] if h == 0 else hid_v[j]
            value = nn(routed, hidden.reshape(z.depth, z.width))
            if not is_first:
                value = value + acc[rows, :]
            if is_last:
                part[rows, :] = value.astype(BF)
            else:
                acc[rows, :] = value
            return carry

        lax.fori_loop(0, z.part // z.mtile, tile, 0)

    def right(first, count):
        for base in range(0, z.width, 512):
            cols = slice(base, min(base + 512, z.width))
            size = cols.stop - cols.start
            wide = nn(rtw[first : first + count].reshape(count * z.cwp, z.wide), part[: z.wide, cols])
            narrow = nn(rtn[first : first + count].reshape(count * z.cnp, z.narrow), part[z.wide :, cols])
            ht[first : first + count, : z.cwp, cols] = wide.astype(BF).reshape(count, z.cwp, size)
            ht[first : first + count, z.cwp :, cols] = narrow.astype(BF).reshape(count, z.cnp, size)

    def chunk(j, is_first=False, is_last=False):
        for h in range(2):
            accumulate(h, j, is_first, is_last)

    plan = [
        (first_arrived,), (0, 1), (1, 1), (second_arrived, 0), (0, 2), (first_far_arrived,),
        (chunk, 0, True), (1, 2), (second_arrived, side - 1), (second_arrived, 1), (0, 3), (1, 3),
        (second_arrived, 2), (0, 4), (chunk, 1), (chunk, side - 1), (1, 4),
        (second_far_arrived, 0), (second_far_arrived, side - 1), (second_far_arrived, 1),
        (0, 5), (second_far_arrived, 2), (1, 5), (chunk, 2, False, True),
    ]
    ringed = []
    for entry in plan:
        if callable(entry[0]):
            entry[0](*entry[1:])
        elif entry[1] <= half:
            gather_step(*entry)
            ringed.append(entry)
    for step in range(1, half + 1):
        for kind in range(2):
            if (kind, step) not in ringed and (kind, step) != (1, half):
                gather_step(kind, step)

    middle = z.seg // 2

    def hops(direction, piece):
        return half if direction == piece else half - 1

    def own_slot(direction, distance):
        return distance if direction == 0 else (n - distance) % n

    def reduce_copy(direction, piece, hop):
        rows = pl.ds(piece * middle, middle)
        if hop == 1:
            src = ht.at[own_slot(direction, hops(direction, piece)), rows]
        else:
            src = land.at[direction, hop - 2, rows]
        return pltpu.make_async_remote_copy(
            src_ref=src, dst_ref=land.at[direction, hop - 1, rows],
            send_sem=rs_send.at[direction, piece, hop - 1],
            recv_sem=rs_recv.at[direction, piece, hop - 1],
            device_id=ring_to[direction], device_id_type=MESH,
        )

    lanes = ((0, 0), (1, 1), (0, 1), (1, 0))
    small = n < 16
    group = n // 4
    start = half - group // 2
    if small:
        right(0, n)
    else:
        right(start, group)
    for direction, piece in lanes:
        if hops(direction, piece) > 0:
            reduce_copy(direction, piece, 1).start()
    if not small:
        right(start + group, group)
        right(start - group, group)

    def reduce_step(hop):
        for direction, piece in lanes:
            if hop >= hops(direction, piece):
                continue
            reduce_copy(direction, piece, hop).wait_recv()
            rows = slice(piece * middle, (piece + 1) * middle)
            slot = own_slot(direction, hops(direction, piece) - hop)
            total = land[direction, hop - 1, rows].astype(F32) + ht[slot, rows].astype(F32)
            land[direction, hop - 1, rows] = total.astype(BF)
            reduce_copy(direction, piece, hop + 1).start()

    def compact(dst, src, count, unit, valid):
        shift = unit.bit_length() - 1
        depth = n * unit

        def tile(m, carry):
            rows = pl.ds(pl.multiple_of(m * z.pick, 16), z.pick)
            feature = lax.broadcasted_iota(jnp.int32, (z.pick, depth), 0) + m * z.pick
            place = lax.broadcasted_iota(jnp.int32, (z.pick, depth), 1)
            owner = (zi + lax.shift_right_logical(place, shift)) & (n - 1)
            inner = place & (unit - 1)
            pick = jnp.where((feature == owner * valid + inner) & (inner < valid), 1.0, 0.0)
            dst[rows, :] = nn(pick.astype(BF), src[...].reshape(depth, src.shape[2])).astype(BF)
            return carry

        lax.fori_loop(0, count // z.pick, tile, 0)

    def compact_left():
        gather_step(1, half)
        compact(lwc, ltw, z.wide, z.cwp, z.cw)
        compact(lnc, ltn, z.narrow, z.cnp, z.cn)

    for hop in range(1, half):
        reduce_step(hop)
        if hop == 1 and not small:
            right(start + 2 * group, n - start - 2 * group)
            right(0, start - group)
        if hop == min(3, half - 1):
            compact_left()
    if half == 1:
        compact_left()

    sums = []
    for piece in range(2):
        rows = slice(piece * middle, (piece + 1) * middle)
        total = ht[0, rows].astype(F32)
        for direction in range(2):
            hop = hops(direction, piece)
            if hop > 0:
                reduce_copy(direction, piece, hop).wait_recv()
                total = total + land[direction, hop - 1, rows].astype(F32)
        sums.append(total.astype(BF))
    final = jnp.concatenate(sums, axis=0)
    upper = nn(final[:, : z.wide], lwc[...])
    lower = nn(final[:, z.wide :], lnc[...])
    ow_ref[:, : z.wide] = upper[: z.cw]
    ow_ref[:, z.wide :] = lower[: z.cw]
    on_ref[:, : z.wide] = upper[z.cwp : z.cwp + z.cn]
    on_ref[:, z.wide :] = lower[z.cwp : z.cwp + z.cn]

    for h in range(2):
        for d in range(2):
            for stage in range(2):
                first_copy(h, stage, d).wait_send()
                for i in range(side):
                    second_copy(h, stage, i, d).wait_send()
        for i in range(side):
            for j in range(side):
                sibling_copy(h, i, j).wait_send()
    for kind in range(2):
        for step in range(1, half + 1):
            for direction in range(2):
                for copy in gather_copies(kind, direction, step):
                    copy.wait_send()
    for direction, piece in lanes:
        for hop in range(1, hops(direction, piece) + 1):
            reduce_copy(direction, piece, hop).wait_send()


def body(
    cotangent, gates, routes, slots, saved_hidden, left_wide, left_narrow, right_wide, right_narrow
):
    ring, experts = lax.axis_size("dp"), lax.axis_size("expert")
    capacity, width = saved_hidden.shape[3:]
    z = Sizes(
        ring, experts, capacity, width, left_wide.shape[1], left_narrow.shape[1],
        cotangent.shape[0], gates.shape[1],
    )
    vmem = pl.BlockSpec(memory_space=pltpu.VMEM)
    ow, on = pl.pallas_call(
        functools.partial(kernel, z),
        out_shape=(
            jax.ShapeDtypeStruct((z.cw, z.width), F32),
            jax.ShapeDtypeStruct((z.cn, z.width), F32),
        ),
        in_specs=[vmem] * 4 + [pl.BlockSpec(memory_space=pl.ANY)] + [vmem] * 4,
        out_specs=(vmem, vmem),
        scratch_shapes=[
            pltpu.VMEM((z.side, z.side, 2, capacity, width), BF),
            pltpu.VMEM((2, z.side, z.side, 2, z.rows, z.tokens), BF),
            pltpu.VMEM((z.depth, z.sources * z.tokens), BF),
            pltpu.VMEM((width, width), F32),
            pltpu.VMEM((width, width), BF),
            pltpu.VMEM((ring, z.cwp, z.wide), BF),
            pltpu.VMEM((ring, z.cnp, z.narrow), BF),
            pltpu.VMEM((ring, z.cwp, z.wide), BF),
            pltpu.VMEM((ring, z.cnp, z.narrow), BF),
            pltpu.VMEM((ring, z.seg, width), BF),
            pltpu.VMEM((2, z.half, z.seg, width), BF),
            pltpu.VMEM((z.wide, z.wide), BF),
            pltpu.VMEM((z.narrow, z.narrow), BF),
            pltpu.SemaphoreType.DMA((experts,)),
            pltpu.SemaphoreType.DMA((2, 2, 2)),
            pltpu.SemaphoreType.DMA((2, 2, 2)),
            pltpu.SemaphoreType.DMA((2, 2, z.side, 2)),
            pltpu.SemaphoreType.DMA((2, 2, z.side, 2)),
            pltpu.SemaphoreType.DMA((2, z.side, z.side)),
            pltpu.SemaphoreType.DMA((2, z.side, z.side)),
            pltpu.SemaphoreType.DMA((2, 2, z.half, 2)),
            pltpu.SemaphoreType.DMA((2, 2, z.half, 2)),
            pltpu.SemaphoreType.DMA((2, 2, z.half)),
            pltpu.SemaphoreType.DMA((2, 2, z.half)),
        ],
        compiler_params=pltpu.CompilerParams(
            collective_id=0, has_side_effects=True, vmem_limit_bytes=60 * 1024 * 1024
        ),
        cost_estimate=pl.CostEstimate(flops=10_000_000_000, bytes_accessed=8_000_000, transcendentals=0),
    )(
        cotangent.T, gates.T, routes.T, slots.T,
        saved_hidden.reshape(experts, capacity, width),
        left_wide[0].T, left_narrow[0].T, right_wide[0].T, right_narrow[0].T,
    )
    return ow.T[None], on.T[None]


def solution(mesh):
    return jax.shard_map(
        body,
        mesh=mesh,
        in_specs=(
            P(("dp", "expert"), None),
            P(("dp", "expert"), None),
            P(("dp", "expert"), None),
            P(("dp", "expert"), None),
            P("dp", "expert", None, None, None),
            P("expert", None, "dp"),
            P("expert", None, "dp"),
            P("expert", None, "dp"),
            P("expert", None, "dp"),
        ),
        out_specs=(P("expert", None, "dp"), P("expert", None, "dp")),
        check_vma=False,
    )
```

time: 159 us -> 141 us (0.89)
  the two profiles are of different devices: /device:TPU:3 before, /device:TPU:24 now
where the time goes in v2:
time: 141 us; the launch traced here: 140 us
  Pallas kernels  135 us (96%)
  local copies, waits for them, and re-layouts  3.9 us (3%)
    pallas_call x1, Pallas kernels, body(): pl.pallas_call(functools.partial(kernel, z), out_shape=(jax.ShapeDtypeStr...  135 us
    unnamed x2, local copies, waits for them, and re-layouts  3.9 us

profile of v2, /device:TPU:24, one launch (start us, length us, event | category | flops | bytes accessed | tf_op | source)
XLA Modules:
  0.0 139.6 jit_solution(16810437439370964335)
XLA Ops:
  0.6 135.1 %shard_map.104 = (f32[60,1440]{1,0:T(8,128)}, f32[30,1440]{1,0:T(8,128)}) custom-call(bf16[1440,128]{1,0:T(8,128)(2,1)} %bitcast.26, bf16[4,128]{1,0:T(4,128)(2,1)} %bitcast.33, s32[4,128]{1,0:T(4,128)} %bitcast.31, s32[4,128]{1,0:T(4,128)} %bitcast.32, bf16[32,32,1440]{2,1,0:T(8,128)(2,1)} %bitcast.25, bf16[60,960]{1,0:T(8,128)(2,1)} %bitcast.27, ...), custom_call_target="tpu_custom_call" | custom-call | flops 10000000000 | bytes 8000000 | tf_op jit(solution)/shard_map/pallas_call | solution.py:416
  135.7 2.1 %copy.11 = f32[1,1440,60]{1,0,2:T(1,128)} copy(f32[1,1440,60]{1,2,0:T(8,128)} %bitcast.23) | data formatting | bytes 691200
  137.8 1.8 %copy.12 = f32[1,1440,30]{1,0,2:T(1,128)} copy(f32[1,1440,30]{1,2,0:T(8,128)} %bitcast.24) | data formatting | bytes 345600

commit v3 on v2

--- a/solution.py
+++ b/solution.py
@@ -41,14 +41,16 @@
         self.rows = self.meta + self.part
         self.sources = 2 * self.side
         self.depth = self.sources * capacity
-        self.mtile = self.part // 3
+        self.rest = width % LANE
+        self.kept = width - self.rest
+        self.tiles = ((0, 512), (512, 1024), (1024, width))
         self.pick = narrow // 2
 
 
 def kernel(
     z, cot_ref, gates_ref, routes_ref, slots_ref, hid_hbm, lw_ref, ln_ref, rw_ref, rn_ref,
     ow_ref, on_ref,
-    hid_v, cg, wt, acc, part, rtw, rtn, ltw, ltn, ht, land, lwc, lnc,
+    hid_v, cg, wt, bt, acc, part, rtw, rtn, ltw, ltn, ht, land, lwc, lnc,
     hid_sem, p_send, p_recv, q_send, q_recv, s_send, s_recv, ag_send, ag_recv, rs_send, rs_recv,
 ):
     n, half, side = z.ring, z.half, z.side
@@ -220,10 +222,10 @@
 
     lax.fori_loop(0, z.experts, hidden_wait, 0)
 
-    def accumulate(h, j, is_first, is_last):
+    def prepare(h, j, place):
         for i in range(side):
             sibling_copy(h, i, j).wait_recv()
-        place = lax.broadcasted_iota(jnp.int32, (z.capacity, z.tokens), 0).astype(F32)
+        slot_row = lax.broadcasted_iota(jnp.int32, (z.capacity, z.tokens), 0).astype(F32)
         mine = ei.astype(F32)
         for s in range(z.sources):
             info = cg[h, s // 2, j, s % 2, : z.meta].astype(F32)
@@ -232,61 +234,95 @@
                 gate = info[k : k + 1]
                 route = info[z.routes + k : z.routes + k + 1]
                 slot = info[2 * z.routes + k : 2 * z.routes + k + 1]
-                weight = weight + jnp.where((route == mine) & (slot == place), gate, 0.0)
+                weight = weight + jnp.where((route == mine) & (slot == slot_row), gate, 0.0)
             wt[
                 s * z.capacity : (s + 1) * z.capacity, s * z.tokens : (s + 1) * z.tokens
             ] = weight.astype(BF)
-
-        def tile(m, carry):
-            inner = pl.ds(pl.multiple_of(z.meta + m * z.mtile, 16), z.mtile)
-            rows = pl.ds(pl.multiple_of(h * z.part + m * z.mtile, 16), z.mtile)
-            left = jnp.concatenate(
-                [cg[h, s // 2, j, s % 2, inner, :] for s in range(z.sources)], axis=1
+        left = jnp.concatenate(
+            [cg[h, s // 2, j, s % 2, z.meta :, :] for s in range(z.sources)], axis=1
+        )
+        bt[:, place * z.depth : (place + 1) * z.depth] = nt(left, wt[...]).astype(BF)
+
+    def add_tile(h, offsets, tile, is_first, is_last):
+        cols = slice(*z.tiles[tile])
+        rows = slice(h * z.part, (h + 1) * z.part)
+        size = cols.stop - cols.start
+        hidden = jnp.concatenate(
+            [(hid_v[:, j, :, :, cols] if h == 0 else hid_v[j, :, :, :, cols]).reshape(z.depth, size)
+             for j in offsets], axis=0,
+        )
+        value = nn(bt[:, : len(offsets) * z.depth], hidden)
+        if not is_first:
+            value = value + acc[rows, cols]
+        if is_last:
+            part[rows, cols] = value.astype(BF)
+        else:
+            acc[rows, cols] = value
+
+    def right(first, count):
+        for buf, unit, valid, lower, rows in (
+            (rtw, z.cwp, z.cw, slice(0, z.wide), slice(0, z.cwp)),
+            (rtn, z.cnp, z.cn, slice(z.wide, z.width), slice(z.cwp, z.seg)),
+        ):
+            left = buf[first : first + count].reshape(count * unit, buf.shape[2])
+            tail = nn(left, part[lower, slice(*z.tiles[2])]).astype(BF)
+            keep = z.kept - z.tiles[2][0]
+            ht[first : first + count, rows, z.tiles[2][0] : z.kept] = tail[:, :keep].reshape(
+                count, unit, keep
             )
-            routed = nt(left, wt[...]).astype(BF)
-            hidden = hid_v[:, j] if h == 0 else hid_v[j]
-            value = nn(routed, hidden.reshape(z.depth, z.width))
-            if not is_first:
-                value = value + acc[rows, :]
-            if is_last:
-                part[rows, :] = value.astype(BF)
-            else:
-                acc[rows, :] = value
-            return carry
-
-        lax.fori_loop(0, z.part // z.mtile, tile, 0)
-
-    def right(first, count):
-        for base in range(0, z.width, 512):
-            cols = slice(base, min(base + 512, z.width))
-            size = cols.stop - cols.start
-            wide = nn(rtw[first : first + count].reshape(count * z.cwp, z.wide), part[: z.wide, cols])
-            narrow = nn(rtn[first : first + count].reshape(count * z.cnp, z.narrow), part[z.wide :, cols])
-            ht[first : first + count, : z.cwp, cols] = wide.astype(BF).reshape(count, z.cwp, size)
-            ht[first : first + count, z.cwp :, cols] = narrow.astype(BF).reshape(count, z.cnp, size)
-
-    def chunk(j, is_first=False, is_last=False):
-        for h in range(2):
-            accumulate(h, j, is_first, is_last)
-
-    plan = [
-        (first_arrived,), (0, 1), (1, 1), (second_arrived, 0), (0, 2), (first_far_arrived,),
-        (chunk, 0, True), (1, 2), (second_arrived, side - 1), (second_arrived, 1), (0, 3), (1, 3),
-        (second_arrived, 2), (0, 4), (chunk, 1), (chunk, side - 1), (1, 4),
-        (second_far_arrived, 0), (second_far_arrived, side - 1), (second_far_arrived, 1),
-        (0, 5), (second_far_arrived, 2), (1, 5), (chunk, 2, False, True),
-    ]
-    ringed = []
-    for entry in plan:
-        if callable(entry[0]):
-            entry[0](*entry[1:])
-        elif entry[1] <= half:
-            gather_step(*entry)
-            ringed.append(entry)
-    for step in range(1, half + 1):
-        for kind in range(2):
-            if (kind, step) not in ringed and (kind, step) != (1, half):
-                gather_step(kind, step)
+            folded = fold(tail[:, keep:], count * unit, unit, valid)
+            for tile in range(2):
+                cols = slice(*z.tiles[tile])
+                value = nn(left, part[lower, cols])
+                if tile == 0:
+                    value = value + folded
+                ht[first : first + count, rows, cols] = value.astype(BF).reshape(
+                    count, unit, cols.stop - cols.start
+                )
+
+    def spread(size):
+        lane = lax.broadcasted_iota(jnp.int32, (z.rest, size), 1)
+        return (lane & (z.rest - 1)) == lax.broadcasted_iota(jnp.int32, (z.rest, size), 0)
+
+    def one(mask):
+        return jnp.where(mask, 1.0, 0.0).astype(BF)
+
+    def fold(rest, count, unit, valid):
+        size = z.tiles[0][1]
+        spare = unit - valid
+        low = spare.bit_length() - 1
+        shift = z.rest.bit_length() - 1
+        wide = nn(rest, one(spread(size)))
+        row = lax.broadcasted_iota(jnp.int32, (count, size), 0)
+        lane = lax.broadcasted_iota(jnp.int32, (count, size), 1)
+        own = lax.shift_right_logical(row & (unit - 1), low) == lax.shift_right_logical(lane, shift)
+        wide = jnp.where(own, wide, 0.0).astype(BF)
+        to = lax.broadcasted_iota(jnp.int32, (count, count), 0)
+        frm = lax.broadcasted_iota(jnp.int32, (count, count), 1)
+        same = (to & -unit) == (frm & -unit)
+        pick = same & ((to & (unit - 1)) - valid == (frm & (spare - 1)))
+        return nn(one(pick), wide)
+
+    def unfold(final):
+        size = z.tiles[0][1]
+        shift = z.rest.bit_length() - 1
+        spare_w, spare_n = z.cwp - z.cw, z.cnp - z.cn
+        low_w, low_n = spare_w.bit_length() - 1, spare_n.bit_length() - 1
+        to = lax.broadcasted_iota(jnp.int32, (z.seg, z.seg), 0)
+        frm = lax.broadcasted_iota(jnp.int32, (z.seg, z.seg), 1)
+        source = jnp.where(
+            to < z.cwp, z.cw + (to & (spare_w - 1)), z.cwp + z.cn + (to & (spare_n - 1))
+        )
+        rows = nn(one(frm == source), final[:, :size])
+        row = lax.broadcasted_iota(jnp.int32, (z.seg, size), 0)
+        lane = lax.broadcasted_iota(jnp.int32, (z.seg, size), 1)
+        place = jnp.where(
+            row < z.cwp,
+            lax.shift_right_logical(row, low_w),
+            lax.shift_right_logical(row - z.cwp, low_n),
+        )
+        rows = jnp.where(place == lax.shift_right_logical(lane, shift), rows, 0.0).astype(BF)
+        return nt(rows, one(spread(size))).astype(BF)
 
     middle = z.seg // 2
 
@@ -309,20 +345,7 @@
             device_id=ring_to[direction], device_id_type=MESH,
         )
 
-    lanes = ((0, 0), (1, 1), (0, 1), (1, 0))
-    small = n < 16
-    group = n // 4
-    start = half - group // 2
-    if small:
-        right(0, n)
-    else:
-        right(start, group)
-    for direction, piece in lanes:
-        if hops(direction, piece) > 0:
-            reduce_copy(direction, piece, 1).start()
-    if not small:
-        right(start + group, group)
-        right(start - group, group)
+    lanes = ((0, 1), (1, 0), (0, 0), (1, 1))
 
     def reduce_step(hop):
         for direction, piece in lanes:
@@ -335,36 +358,71 @@
             land[direction, hop - 1, rows] = total.astype(BF)
             reduce_copy(direction, piece, hop + 1).start()
 
-    def compact(dst, src, count, unit, valid):
+    def compact(dst, src, unit, valid, m):
         shift = unit.bit_length() - 1
         depth = n * unit
-
-        def tile(m, carry):
-            rows = pl.ds(pl.multiple_of(m * z.pick, 16), z.pick)
-            feature = lax.broadcasted_iota(jnp.int32, (z.pick, depth), 0) + m * z.pick
-            place = lax.broadcasted_iota(jnp.int32, (z.pick, depth), 1)
-            owner = (zi + lax.shift_right_logical(place, shift)) & (n - 1)
-            inner = place & (unit - 1)
-            pick = jnp.where((feature == owner * valid + inner) & (inner < valid), 1.0, 0.0)
-            dst[rows, :] = nn(pick.astype(BF), src[...].reshape(depth, src.shape[2])).astype(BF)
-            return carry
-
-        lax.fori_loop(0, count // z.pick, tile, 0)
-
-    def compact_left():
-        gather_step(1, half)
-        compact(lwc, ltw, z.wide, z.cwp, z.cw)
-        compact(lnc, ltn, z.narrow, z.cnp, z.cn)
-
+        rows = slice(m * z.pick, (m + 1) * z.pick)
+        feature = lax.broadcasted_iota(jnp.int32, (z.pick, depth), 0) + m * z.pick
+        place = lax.broadcasted_iota(jnp.int32, (z.pick, depth), 1)
+        owner = (zi + lax.shift_right_logical(place, shift)) & (n - 1)
+        inner = place & (unit - 1)
+        pick = one((feature == owner * valid + inner) & (inner < valid))
+        dst[rows, :] = nn(pick, src[...].reshape(depth, src.shape[2])).astype(BF)
+
+    def work(h, offsets, is_first=False, is_last=False):
+        for place, j in enumerate(offsets):
+            prepare(h, j, place)
+            yield
+        for tile in range(3):
+            add_tile(h, offsets, tile, is_first, is_last)
+            yield
+
+    def run(*steps):
+        for entry in steps:
+            if isinstance(entry, int):
+                for _ in range(entry):
+                    next(jobs, None)
+            else:
+                entry[0](*entry[1:])
+
+    def all_work():
+        for h in range(2):
+            yield from work(h, (0,), is_first=True)
+        for h in range(2):
+            yield from work(h, (1, side - 1))
+        for h in range(2):
+            yield from work(h, (2,), is_last=True)
+
+    jobs = all_work()
+    far = side - 1
+    ring = gather_step
+    run(
+        (ring, 0, 1), (first_arrived,), (ring, 1, 1), (second_arrived, 0), (ring, 0, 2),
+        (first_far_arrived,), 1, (ring, 1, 2), 3, (second_arrived, far), (ring, 0, 3), 3,
+        (ring, 1, 3), 1, (second_arrived, 1), (ring, 0, 4), (second_arrived, 2), (ring, 1, 4),
+        (second_far_arrived, 0), 2, (ring, 0, 5), (second_far_arrived, far), 3, (ring, 1, 5),
+        (second_far_arrived, 1), 2, (ring, 0, 6), (second_far_arrived, 2), 3, (ring, 1, 6), 4,
+        (ring, 0, 7), 4,
+    )
+    right(0, half)
+    reduce_copy(0, 1, 1).start()
+    gather_step(1, half - 1)
+    right(half + 1, n - half - 1)
+    reduce_copy(1, 0, 1).start()
+    gather_step(0, half)
+    right(half, 1)
+    reduce_copy(0, 0, 1).start()
+    reduce_copy(1, 1, 1).start()
+    gather_step(1, half)
+
+    later = [(lwc, ltw, z.cwp, z.cw, m) for m in range(z.wide // z.pick)]
+    later += [(lnc, ltn, z.cnp, z.cn, m) for m in range(z.narrow // z.pick)]
     for hop in range(1, half):
         reduce_step(hop)
-        if hop == 1 and not small:
-            right(start + 2 * group, n - start - 2 * group)
-            right(0, start - group)
-        if hop == min(3, half - 1):
-            compact_left()
-    if half == 1:
-        compact_left()
+        if hop >= 2 and later:
+            compact(*later.pop(0))
+    for entry in later:
+        compact(*entry)
 
     sums = []
     for piece in range(2):
@@ -378,11 +436,10 @@
         sums.append(total.astype(BF))
     final = jnp.concatenate(sums, axis=0)
     upper = nn(final[:, : z.wide], lwc[...])
-    lower = nn(final[:, z.wide :], lnc[...])
-    ow_ref[:, : z.wide] = upper[: z.cw]
-    ow_ref[:, z.wide :] = lower[: z.cw]
-    on_ref[:, : z.wide] = upper[z.cwp : z.cwp + z.cn]
-    on_ref[:, z.wide :] = lower[z.cwp : z.cwp + z.cn]
+    lower = nn(final[:, z.wide :], lnc[: z.kept - z.wide]) + nn(unfold(final), lnc[z.kept - z.wide :])
+    result = jnp.concatenate([upper, lower], axis=1)
+    ow_ref[:, 0, :] = result[: z.cw]
+    on_ref[:, 0, :] = result[z.cwp : z.cwp + z.cn]
 
     for h in range(2):
         for d in range(2):
@@ -416,8 +473,8 @@
     ow, on = pl.pallas_call(
         functools.partial(kernel, z),
         out_shape=(
-            jax.ShapeDtypeStruct((z.cw, z.width), F32),
-            jax.ShapeDtypeStruct((z.cn, z.width), F32),
+            jax.ShapeDtypeStruct((z.cw, 1, z.width), F32),
+            jax.ShapeDtypeStruct((z.cn, 1, z.width), F32),
         ),
         in_specs=[vmem] * 4 + [pl.BlockSpec(memory_space=pl.ANY)] + [vmem] * 4,
         out_specs=(vmem, vmem),
@@ -425,14 +482,15 @@
             pltpu.VMEM((z.side, z.side, 2, capacity, width), BF),
             pltpu.VMEM((2, z.side, z.side, 2, z.rows, z.tokens), BF),
             pltpu.VMEM((z.depth, z.sources * z.tokens), BF),
+            pltpu.VMEM((z.part, 2 * z.depth), BF),
             pltpu.VMEM((width, width), F32),
             pltpu.VMEM((width, width), BF),
             pltpu.VMEM((ring, z.cwp, z.wide), BF),
             pltpu.VMEM((ring, z.cnp, z.narrow), BF),
             pltpu.VMEM((ring, z.cwp, z.wide), BF),
             pltpu.VMEM((ring, z.cnp, z.narrow), BF),
-            pltpu.VMEM((ring, z.seg, width), BF),
-            pltpu.VMEM((2, z.half, z.seg, width), BF),
+            pltpu.VMEM((ring, z.seg, z.kept), BF),
+            pltpu.VMEM((2, z.half, z.seg, z.kept), BF),
             pltpu.VMEM((z.wide, z.wide), BF),
             pltpu.VMEM((z.narrow, z.narrow), BF),
             pltpu.SemaphoreType.DMA((experts,)),
@@ -456,7 +514,7 @@
         saved_hidden.reshape(experts, capacity, width),
         left_wide[0].T, left_narrow[0].T, right_wide[0].T, right_narrow[0].T,
     )
-    return ow.T[None], on.T[None]
+    return jnp.transpose(ow, (1, 2, 0)), jnp.transpose(on, (1, 2, 0))
 
 
 def solution(mesh):

time: 141 us -> 129 us (0.915)
  Pallas kernels: 135 us -> 123 us
    pallas_call x1, Pallas kernels: 135 us -> 123 us  [body(): pl.pallas_call(functools.partial(kernel, z), out_shape=(jax.ShapeDtypeStr...]
where the time goes in v3:
time: 129 us; the launch traced here: 127 us
  Pallas kernels  123 us (95%)
  local copies, waits for them, and re-layouts  3.38 us (3%)
    pallas_call x1, Pallas kernels, body(): pl.pallas_call(functools.partial(kernel, z), out_shape=(jax.ShapeDtypeStr...  123 us
    unnamed x2, local copies, waits for them, and re-layouts  3.38 us

profile of v3, /device:TPU:24, one launch (start us, length us, event | category | flops | bytes accessed | tf_op | source)
XLA Modules:
  0.0 126.8 jit_solution(6299518165669499954)
XLA Ops:
  0.6 122.8 %shard_map.104 = (f32[60,1,1440]{2,1,0:T(1,128)}, f32[30,1,1440]{2,1,0:T(1,128)}) custom-call(bf16[1440,128]{1,0:T(8,128)(2,1)} %bitcast.22, bf16[4,128]{1,0:T(4,128)(2,1)} %bitcast.29, s32[4,128]{1,0:T(4,128)} %bitcast.27, s32[4,128]{1,0:T(4,128)} %bitcast.28, bf16[32,32,1440]{2,1,0:T(8,128)(2,1)} %bitcast.21, bf16[60,960]{1,0:T(8,128)(2,1)} %bitcast.23, ...), custom_call_target="tpu_custom_call" | custom-call | flops 10000000000 | bytes 8000000 | tf_op jit(solution)/shard_map/pallas_call | solution.py:473
  123.4 1.8 %copy.13 = f32[1,1440,60]{1,0,2:T(1,128)} copy(f32[1,1440,60]{1,0,2:T(1,128)} %bitcast.19) | data formatting | bytes 691200
  125.2 1.6 %copy.14 = f32[1,1440,30]{1,0,2:T(1,128)} copy(f32[1,1440,30]{1,0,2:T(1,128)} %bitcast.20) | data formatting | bytes 345600

commit v4 on v3

--- a/solution.py
+++ b/solution.py
@@ -45,12 +45,18 @@
         self.kept = width - self.rest
         self.tiles = ((0, 512), (512, 1024), (1024, width))
         self.pick = narrow // 2
+        self.beside = 2 * narrow // 5
+        self.tail = narrow - 2 * self.beside
+        self.packed = wide + self.beside
+        self.spare = self.cwp - self.cw
+        self.folds = self.cnp // self.spare
+        self.folded = self.folds * self.tail
 
 
 def kernel(
     z, cot_ref, gates_ref, routes_ref, slots_ref, hid_hbm, lw_ref, ln_ref, rw_ref, rn_ref,
     ow_ref, on_ref,
-    hid_v, cg, wt, bt, acc, part, rtw, rtn, ltw, ltn, ht, land, lwc, lnc,
+    hid_v, cg, wt, bt, acc, part, rtp, rtn, ltp, ltn, spr, ht, land, lwc, lnc,
     hid_sem, p_send, p_recv, q_send, q_recv, s_send, s_recv, ag_send, ag_recv, rs_send, rs_recv,
 ):
     n, half, side = z.ring, z.half, z.side
@@ -76,6 +82,15 @@
     for target in (*ring_to, *x_to, *y_to, sibling):
         pl.semaphore_signal(barrier, inc=1, device_id=target, device_id_type=MESH)
 
+    def one(mask):
+        return jnp.where(mask, 1.0, 0.0).astype(BF)
+
+    def in_fold(count):
+        row = lax.broadcasted_iota(jnp.int32, (count, z.folded), 0) & (z.cnp - 1)
+        lane = lax.broadcasted_iota(jnp.int32, (count, z.folded), 1)
+        low = lax.shift_right_logical(row, z.spare.bit_length() - 1) * z.tail
+        return (lane >= low) & (lane < low + z.tail)
+
     def hidden_copy(k):
         dx, dy, dc = k // (2 * side), lax.rem(k // 2, side), lax.rem(k, 2)
         source = expert_at(
@@ -89,11 +104,25 @@
 
     lax.fori_loop(0, z.experts, hidden_start, 0)
 
-    for dst, src, rows in (
-        (rtw, rw_ref, z.cw), (rtn, rn_ref, z.cn), (ltw, lw_ref, z.cw), (ltn, ln_ref, z.cn)
-    ):
+    lane = lax.broadcasted_iota(jnp.int32, (z.tail, z.folded), 1)
+    base = lax.broadcasted_iota(jnp.int32, (z.tail, z.folded), 0)
+    hit = lane == base
+    for k in range(1, z.folds):
+        hit = hit | (lane == base + k * z.tail)
+    spr[...] = one(hit)
+    for dst, wide_src, narrow_src in ((rtp, rw_ref, rn_ref), (ltp, lw_ref, ln_ref)):
         dst[0] = jnp.zeros(dst.shape[1:], BF)
-        dst[0, :rows] = src[...]
+        dst[0, : z.cw, : z.wide] = wide_src[...]
+        dst[0, : z.cn, z.wide :] = narrow_src[:, : z.beside]
+        dst[0, z.cnp : z.cnp + z.cn, z.wide :] = narrow_src[:, z.beside : 2 * z.beside]
+        rest = jnp.concatenate(
+            [narrow_src[:, 2 * z.beside :].astype(F32), jnp.zeros((z.cnp - z.cn, z.tail), F32)], axis=0
+        ).astype(BF)
+        kept = jnp.where(in_fold(z.cnp), nn(rest, spr[...]), 0.0).astype(BF)
+        to = lax.broadcasted_iota(jnp.int32, (z.cwp, z.cnp), 0)
+        frm = lax.broadcasted_iota(jnp.int32, (z.cwp, z.cnp), 1)
+        spare_rows = nn(one(to == z.cw + (frm & (z.spare - 1))), kept)
+        dst[0, :, : z.folded] = (dst[0, :, : z.folded].astype(F32) + spare_rows).astype(BF)
     spare = jnp.zeros((z.meta - 3 * z.routes, z.tokens), F32)
     meta = jnp.concatenate(
         [gates_ref[...].astype(F32), routes_ref[...].astype(F32), slots_ref[...].astype(F32), spare],
@@ -108,7 +137,7 @@
 
     def gather_copies(kind, direction, step):
         copies = []
-        for piece, buf in enumerate(((rtw, rtn), (ltw, ltn))[kind]):
+        for piece, buf in enumerate(((rtp,), (ltp,))[kind]):
             if direction == 0:
                 src, dst = (n - step + 1) % n, n - step
             else:
@@ -259,12 +288,31 @@
         else:
             acc[rows, cols] = value
 
+    def unpack(kind, first, count):
+        src, dst = ((rtp, rtn), (ltp, ltn))[kind]
+        some = slice(first, first + count)
+        dst[some, :, : z.beside] = src[some, : z.cnp, z.wide :]
+        dst[some, :, z.beside : 2 * z.beside] = src[some, z.cnp :, z.wide :]
+        to = lax.broadcasted_iota(jnp.int32, (count * z.cnp, count * z.cwp), 0)
+        frm = lax.broadcasted_iota(jnp.int32, (count * z.cnp, count * z.cwp), 1)
+        same = lax.shift_right_logical(to, z.cnp.bit_length() - 1) == lax.shift_right_logical(
+            frm, z.cwp.bit_length() - 1
+        )
+        pick = same & ((frm & (z.cwp - 1)) == z.cw + (to & (z.spare - 1)))
+        rows = nn(one(pick), src[some, :, : z.folded].reshape(count * z.cwp, z.folded))
+        rows = jnp.where(in_fold(count * z.cnp), rows, 0.0).astype(BF)
+        dst[some, :, 2 * z.beside :] = nt(rows, spr[...]).astype(BF).reshape(count, z.cnp, z.tail)
+
     def right(first, count):
         for buf, unit, valid, lower, rows in (
-            (rtw, z.cwp, z.cw, slice(0, z.wide), slice(0, z.cwp)),
+            (rtp, z.cwp, z.cw, slice(0, z.wide), slice(0, z.cwp)),
             (rtn, z.cnp, z.cn, slice(z.wide, z.width), slice(z.cwp, z.seg)),
         ):
-            left = buf[first : first + count].reshape(count * unit, buf.shape[2])
+            depth = lower.stop - lower.start
+            left = buf[first : first + count, :, :depth].reshape(count * unit, depth)
+            if buf is rtp:
+                row = lax.broadcasted_iota(jnp.int32, (count * unit, depth), 0) & (unit - 1)
+                left = jnp.where(row < valid, left.astype(F32), 0.0).astype(BF)
             tail = nn(left, part[lower, slice(*z.tiles[2])]).astype(BF)
             keep = z.kept - z.tiles[2][0]
             ht[first : first + count, rows, z.tiles[2][0] : z.kept] = tail[:, :keep].reshape(
@@ -283,9 +331,6 @@
     def spread(size):
         lane = lax.broadcasted_iota(jnp.int32, (z.rest, size), 1)
         return (lane & (z.rest - 1)) == lax.broadcasted_iota(jnp.int32, (z.rest, size), 0)
-
-    def one(mask):
-        return jnp.where(mask, 1.0, 0.0).astype(BF)
 
     def fold(rest, count, unit, valid):
         size = z.tiles[0][1]
@@ -367,7 +412,8 @@
         owner = (zi + lax.shift_right_logical(place, shift)) & (n - 1)
         inner = place & (unit - 1)
         pick = one((feature == owner * valid + inner) & (inner < valid))
-        dst[rows, :] = nn(pick, src[...].reshape(depth, src.shape[2])).astype(BF)
+        width = dst.shape[1]
+        dst[rows, :] = nn(pick, src[:, :, :width].reshape(depth, width)).astype(BF)
 
     def work(h, offsets, is_first=False, is_last=False):
         for place, j in enumerate(offsets):
@@ -399,26 +445,31 @@
     run(
         (ring, 0, 1), (first_arrived,), (ring, 1, 1), (second_arrived, 0), (ring, 0, 2),
         (first_far_arrived,), 1, (ring, 1, 2), 3, (second_arrived, far), (ring, 0, 3), 3,
-        (ring, 1, 3), 1, (second_arrived, 1), (ring, 0, 4), (second_arrived, 2), (ring, 1, 4),
+        (ring, 1, 3), 1, (second_arrived, 1), (ring, 0, 4), (unpack, 0, 0, 4), (second_arrived, 2),
+        (ring, 1, 4), (unpack, 0, 12, 4),
         (second_far_arrived, 0), 2, (ring, 0, 5), (second_far_arrived, far), 3, (ring, 1, 5),
         (second_far_arrived, 1), 2, (ring, 0, 6), (second_far_arrived, 2), 3, (ring, 1, 6), 4,
-        (ring, 0, 7), 4,
+        (ring, 0, 7), (unpack, 0, 4, 4), 4,
     )
     right(0, half)
     reduce_copy(0, 1, 1).start()
     gather_step(1, half - 1)
+    unpack(0, half + 1, 3)
     right(half + 1, n - half - 1)
     reduce_copy(1, 0, 1).start()
     gather_step(0, half)
+    unpack(0, half, 1)
     right(half, 1)
     reduce_copy(0, 0, 1).start()
     reduce_copy(1, 1, 1).start()
     gather_step(1, half)
 
-    later = [(lwc, ltw, z.cwp, z.cw, m) for m in range(z.wide // z.pick)]
+    later = [(lwc, ltp, z.cwp, z.cw, m) for m in range(z.wide // z.pick)]
     later += [(lnc, ltn, z.cnp, z.cn, m) for m in range(z.narrow // z.pick)]
     for hop in range(1, half):
         reduce_step(hop)
+        if hop < 3:
+            unpack(1, (hop - 1) * half, half)
         if hop >= 2 and later:
             compact(*later.pop(0))
     for entry in later:
@@ -485,10 +536,11 @@
             pltpu.VMEM((z.part, 2 * z.depth), BF),
             pltpu.VMEM((width, width), F32),
             pltpu.VMEM((width, width), BF),
-            pltpu.VMEM((ring, z.cwp, z.wide), BF),
+            pltpu.VMEM((ring, z.cwp, z.packed), BF),
             pltpu.VMEM((ring, z.cnp, z.narrow), BF),
-            pltpu.VMEM((ring, z.cwp, z.wide), BF),
+            pltpu.VMEM((ring, z.cwp, z.packed), BF),
             pltpu.VMEM((ring, z.cnp, z.narrow), BF),
+            pltpu.VMEM((z.tail, z.folded), BF),
             pltpu.VMEM((ring, z.seg, z.kept), BF),
             pltpu.VMEM((2, z.half, z.seg, z.kept), BF),
             pltpu.VMEM((z.wide, z.wide), BF),
@@ -500,8 +552,8 @@
             pltpu.SemaphoreType.DMA((2, 2, z.side, 2)),
             pltpu.SemaphoreType.DMA((2, z.side, z.side)),
             pltpu.SemaphoreType.DMA((2, z.side, z.side)),
-            pltpu.SemaphoreType.DMA((2, 2, z.half, 2)),
-            pltpu.SemaphoreType.DMA((2, 2, z.half, 2)),
+            pltpu.SemaphoreType.DMA((2, 2, z.half, 1)),
+            pltpu.SemaphoreType.DMA((2, 2, z.half, 1)),
             pltpu.SemaphoreType.DMA((2, 2, z.half)),
             pltpu.SemaphoreType.DMA((2, 2, z.half)),
         ],

time: 129 us -> 124 us (0.961); the launches traced: 127 us -> 124 us
  Pallas kernels: 123 us -> 120 us
    pallas_call x1, Pallas kernels: 123 us -> 120 us  [body(): pl.pallas_call(functools.partial(kernel, z), out_shape=(jax.ShapeDtypeStr...]
where the time goes in v4:
time: 124 us
  Pallas kernels  120 us (97%)
  local copies, waits for them, and re-layouts  3.38 us (3%)
    pallas_call x1, Pallas kernels, body(): pl.pallas_call(functools.partial(kernel, z), out_shape=(jax.ShapeDtypeStr...  120 us
    unnamed x2, local copies, waits for them, and re-layouts  3.38 us

profile of v4, /device:TPU:24, one launch (start us, length us, event | category | flops | bytes accessed | tf_op | source)
XLA Modules:
  0.0 124.0 jit_solution(2401005631314891529)
XLA Ops:
  0.6 120.0 %shard_map.104 = (f32[60,1,1440]{2,1,0:T(1,128)}, f32[30,1,1440]{2,1,0:T(1,128)}) custom-call(bf16[1440,128]{1,0:T(8,128)(2,1)} %bitcast.22, bf16[4,128]{1,0:T(4,128)(2,1)} %bitcast.29, s32[4,128]{1,0:T(4,128)} %bitcast.27, s32[4,128]{1,0:T(4,128)} %bitcast.28, bf16[32,32,1440]{2,1,0:T(8,128)(2,1)} %bitcast.21, bf16[60,960]{1,0:T(8,128)(2,1)} %bitcast.23, ...), custom_call_target="tpu_custom_call" | custom-call | flops 10000000000 | bytes 8000000 | tf_op jit(solution)/shard_map/pallas_call | solution.py:524
  120.6 1.8 %copy.13 = f32[1,1440,60]{1,0,2:T(1,128)} copy(f32[1,1440,60]{1,0,2:T(1,128)} %bitcast.19) | data formatting | bytes 691200
  122.4 1.6 %copy.14 = f32[1,1440,30]{1,0,2:T(1,128)} copy(f32[1,1440,30]{1,0,2:T(1,128)} %bitcast.20) | data formatting | bytes 345600

commit v5 on v4

--- a/solution.py
+++ b/solution.py
@@ -443,13 +443,19 @@
     far = side - 1
     ring = gather_step
     run(
-        (ring, 0, 1), (first_arrived,), (ring, 1, 1), (second_arrived, 0), (ring, 0, 2),
-        (first_far_arrived,), 1, (ring, 1, 2), 3, (second_arrived, far), (ring, 0, 3), 3,
-        (ring, 1, 3), 1, (second_arrived, 1), (ring, 0, 4), (unpack, 0, 0, 4), (second_arrived, 2),
-        (ring, 1, 4), (unpack, 0, 12, 4),
-        (second_far_arrived, 0), 2, (ring, 0, 5), (second_far_arrived, far), 3, (ring, 1, 5),
-        (second_far_arrived, 1), 2, (ring, 0, 6), (second_far_arrived, 2), 3, (ring, 1, 6), 4,
-        (ring, 0, 7), (unpack, 0, 4, 4), 4,
+        (ring, 0, 1),
+        (ring, 1, 1), (first_arrived,),
+        (ring, 0, 2), (second_arrived, 0),
+        (ring, 1, 2), (first_far_arrived,), 3,
+        (ring, 0, 3), (second_arrived, far), 3,
+        (ring, 1, 3), 2,
+        (ring, 0, 4), (unpack, 0, 0, 4), (second_arrived, 1),
+        (ring, 1, 4), (unpack, 0, 12, 4), (second_arrived, 2), 3,
+        (ring, 0, 5), (second_far_arrived, 0), 3,
+        (ring, 1, 5), (second_far_arrived, far), 3,
+        (ring, 0, 6), (second_far_arrived, 1), 1,
+        (ring, 1, 6), (second_far_arrived, 2), 5,
+        (ring, 0, 7), (unpack, 0, 4, 4), 3,
     )
     right(0, half)
     reduce_copy(0, 1, 1).start()

time: 124 us -> 125 us (level); the launches traced: 124 us -> 124 us
  no operation moved by 1% of the time
where the time goes in v5:
time: 125 us; the launch traced here: 124 us
  Pallas kernels  120 us (96%)
  local copies, waits for them, and re-layouts  3.38 us (3%)
    pallas_call x1, Pallas kernels, body(): pl.pallas_call(functools.partial(kernel, z), out_shape=(jax.ShapeDtypeStr...  120 us
    unnamed x2, local copies, waits for them, and re-layouts  3.38 us

profile of v5, /device:TPU:24, one launch (start us, length us, event | category | flops | bytes accessed | tf_op | source)
XLA Modules:
  0.0 123.6 jit_solution(5152493061163466215)
XLA Ops:
  0.6 119.6 %shard_map.104 = (f32[60,1,1440]{2,1,0:T(1,128)}, f32[30,1,1440]{2,1,0:T(1,128)}) custom-call(bf16[1440,128]{1,0:T(8,128)(2,1)} %bitcast.22, bf16[4,128]{1,0:T(4,128)(2,1)} %bitcast.29, s32[4,128]{1,0:T(4,128)} %bitcast.27, s32[4,128]{1,0:T(4,128)} %bitcast.28, bf16[32,32,1440]{2,1,0:T(8,128)(2,1)} %bitcast.21, bf16[60,960]{1,0:T(8,128)(2,1)} %bitcast.23, ...), custom_call_target="tpu_custom_call" | custom-call | flops 10000000000 | bytes 8000000 | tf_op jit(solution)/shard_map/pallas_call | solution.py:530
  120.2 1.8 %copy.13 = f32[1,1440,60]{1,0,2:T(1,128)} copy(f32[1,1440,60]{1,0,2:T(1,128)} %bitcast.19) | data formatting | bytes 691200
  122.0 1.6 %copy.14 = f32[1,1440,30]{1,0,2:T(1,128)} copy(f32[1,1440,30]{1,0,2:T(1,128)} %bitcast.20) | data formatting | bytes 345600

commit v6 on v4

--- a/solution.py
+++ b/solution.py
@@ -451,25 +451,23 @@
         (second_far_arrived, 1), 2, (ring, 0, 6), (second_far_arrived, 2), 3, (ring, 1, 6), 4,
         (ring, 0, 7), (unpack, 0, 4, 4), 4,
     )
-    right(0, half)
-    reduce_copy(0, 1, 1).start()
+    gather_step(0, half)
+    unpack(0, half, 4)
     gather_step(1, half - 1)
-    unpack(0, half + 1, 3)
-    right(half + 1, n - half - 1)
-    reduce_copy(1, 0, 1).start()
-    gather_step(0, half)
-    unpack(0, half, 1)
-    right(half, 1)
-    reduce_copy(0, 0, 1).start()
-    reduce_copy(1, 1, 1).start()
+    right(half - 2, 5)
+    for direction, piece in lanes:
+        reduce_copy(direction, piece, 1).start()
     gather_step(1, half)
+    right(half + 3, n - half - 3)
 
     later = [(lwc, ltp, z.cwp, z.cw, m) for m in range(z.wide // z.pick)]
     later += [(lnc, ltn, z.cnp, z.cn, m) for m in range(z.narrow // z.pick)]
     for hop in range(1, half):
         reduce_step(hop)
-        if hop < 3:
-            unpack(1, (hop - 1) * half, half)
+        if hop == 1:
+            right(0, half - 2)
+        if 1 < hop < 4:
+            unpack(1, (hop - 2) * half, half)
         if hop >= 2 and later:
             compact(*later.pop(0))
     for entry in later:

time: 124 us -> 124 us (level)
  no operation moved by 1% of the time
where the time goes in v6:
time: 124 us
  Pallas kernels  120 us (97%)
  local copies, waits for them, and re-layouts  3.38 us (3%)
    pallas_call x1, Pallas kernels, body(): pl.pallas_call(functools.partial(kernel, z), out_shape=(jax.ShapeDtypeStr...  120 us
    unnamed x2, local copies, waits for them, and re-layouts  3.38 us

profile of v6, /device:TPU:24, one launch (start us, length us, event | category | flops | bytes accessed | tf_op | source)
XLA Modules:
  0.0 123.5 jit_solution(4943044431215897741)
XLA Ops:
  0.6 119.5 %shard_map.104 = (f32[60,1,1440]{2,1,0:T(1,128)}, f32[30,1,1440]{2,1,0:T(1,128)}) custom-call(bf16[1440,128]{1,0:T(8,128)(2,1)} %bitcast.22, bf16[4,128]{1,0:T(4,128)(2,1)} %bitcast.29, s32[4,128]{1,0:T(4,128)} %bitcast.27, s32[4,128]{1,0:T(4,128)} %bitcast.28, bf16[32,32,1440]{2,1,0:T(8,128)(2,1)} %bitcast.21, bf16[60,960]{1,0:T(8,128)(2,1)} %bitcast.23, ...), custom_call_target="tpu_custom_call" | custom-call | flops 10000000000 | bytes 8000000 | tf_op jit(solution)/shard_map/pallas_call | solution.py:522
  120.2 1.8 %copy.13 = f32[1,1440,60]{1,0,2:T(1,128)} copy(f32[1,1440,60]{1,0,2:T(1,128)} %bitcast.19) | data formatting | bytes 691200
  121.9 1.6 %copy.14 = f32[1,1440,30]{1,0,2:T(1,128)} copy(f32[1,1440,30]{1,0,2:T(1,128)} %bitcast.20) | data formatting | bytes 345600
